TPU v7x, 32 devices: a whole 2x2x4 slice. The times are simulated.
32 devices in a mesh: seq: 4 (over y, x), dec: 8 (over z, core).
Axes of the slice: x: 2, y: 2, z: 4, core: 2. Of those that a mesh axis runs over, the one named last changes fastest.
Arguments:
- latents: bfloat16 [4, 4, 12, 8, 1024], P('seq', None, None, 'dec'), may hold values from -6 to 6
- cache_lat: bfloat16 [4, 4, 12, 8, 512], P('seq', None, None, 'dec'), may hold values from -6 to 6
- cache_act: bfloat16 [4, 4, 12, 8, 12288], P('seq', None, None, 'dec'), may hold values from -0.25 to 2
- w_in: bfloat16 [27, 16, 384], replicated, may hold values from -0.3125 to 0.3125
- w_mid: bfloat16 [27, 384, 384], replicated, may hold values from -0.0625 to 0.0625
- norm_gain: float32 [384], replicated, may hold values from 0.1 to 1.9
- clip_group: int32 [4, 4], replicated, may hold values from 0 to 3, as said below
- band_rows: int32 [4, 8], replicated, may hold values from 2 to 96, as said below
Outputs:
- decoded: bfloat16 [4, 8, 96, 4, 16, 384], P('seq', 'dec')
Inputs may be any that keep to these rules, and one draw needn't show every extreme that they name: For every sequence shard s, clip_group[s, :] names each of the 4 groups once. Each row of band_rows sums to 384; every band has 2 rows or more, and in each row one band has exactly 96 rows.
All inputs are finite; a program needn't handle non-finite values.
Results may differ from a plain program's by a relative error of at most 0.0029.
Values may be sent and summed in bfloat16 or wider, within the bound.
No kernel may reach another device: no remote copies, remote signals or barrier semaphores. Data moves between devices by JAX's collectives and lax.ppermute only.
A program may use at most 384 MiB of HBM per device.

v0:
```python
import functools

import jax
import jax.numpy as jnp
from jax import lax
from jax.experimental import pallas as pl
from jax.experimental.pallas import tpu as pltpu
from jax.sharding import PartitionSpec as P

F = 4
CT = 2
COLS = 16
LANES = 128
EPSILON = 1e-06
F32 = jnp.float32
BF16 = jnp.bfloat16


def band_start(bands, group, owner, owners):
    total = jnp.int32(0)
    for other in range(owners):
        total = total + jnp.where(other < owner, bands[group, other], 0)
    return total


def first_unit(start, margin, source, owners, units, capacity):
    unit = (start - margin - source + owners - 1 + 2 * owners) // owners - 2
    return jnp.clip(unit, 0, units - capacity)


def clip_of(groups_ref, shard, group, clips):
    found = jnp.int32(0)
    for clip in range(clips):
        found = found + jnp.where(groups_ref[shard, clip] == group, clip, 0)
    return found


def pack_clips(groups_ref, lat_in, old_in, act_in, *refs, per_owner, per_step, clips):
    *outs, lat_ref, old_ref, act_ref, lat_scratch, act_scratch, sems = refs
    shard = lax.axis_index("seq")
    copies = [
        pltpu.make_async_copy(lat_in, lat_ref, sems.at[0]),
        pltpu.make_async_copy(old_in, old_ref, sems.at[1]),
    ]
    steps = per_owner // per_step
    for step in range(steps):
        rows = pl.ds(step * per_step, per_step)
        copies.append(
            pltpu.make_async_copy(act_in.at[rows], act_ref.at[rows], sems.at[2 + step])
        )
    for copy in copies:
        copy.start()
    chosen = [clip_of(groups_ref, shard, shard ^ other, clips) for other in range(clips)]
    tiles = act_ref.shape[2] // LANES
    depth = tiles // (CT * COLS)
    size = per_step * tiles
    lat_rows = outs[0].shape[0] - per_owner * tiles
    copies[0].wait()
    copies[1].wait()
    for row in range(per_owner):
        for frame in range(CT + F):
            for half in range(2):
                if frame < CT:
                    tile = frame * 2 + half
                    value = old_ref[row, :, tile * LANES : (tile + 1) * LANES]
                else:
                    tile = (frame - CT) * 2 + half
                    value = lat_ref[row, :, tile * LANES : (tile + 1) * LANES]
                at = row * 12 + half * (CT + F) + frame
                lat_scratch[pl.ds(at, clips, stride=lat_rows), :] = value.astype(F32)
    for out, clip in zip(outs, chosen):
        rows = pl.ds(pl.multiple_of(clip * lat_rows, 8), lat_rows)
        out[per_owner * tiles :, :] = lat_scratch[rows, :].astype(BF16)
    for step in range(steps):
        copies[2 + step].wait()
        for row in range(per_step):
            for frame in range(CT):
                for col in range(COLS):
                    for part in range(depth):
                        tile = (frame * COLS + col) * depth + part
                        at = row * tiles + (frame * depth + part) * COLS + col
                        value = act_ref[
                            step * per_step + row, :, tile * LANES : (tile + 1) * LANES
                        ]
                        act_scratch[step % 2, pl.ds(at, clips, stride=size), :] = value.astype(F32)
        for out, clip in zip(outs, chosen):
            rows = pl.ds(pl.multiple_of(clip * size, 8), size)
            out[step * size : (step + 1) * size, :] = act_scratch[step % 2, rows, :].astype(BF16)


def slice_bands(
    bands, _, *refs, owners, units, lat_capacity, act_capacity, per_owner, tiles, groups
):
    ins, lat_outs, act_outs = refs[:groups], refs[groups : groups + owners], refs[groups + owners : -4]
    lat_scratch, scratch, in_sems, sems = refs[-4:]
    group = lax.axis_index("seq")
    source = lax.axis_index("dec")
    size = per_owner * tiles
    copies = []
    for other, in_ref in enumerate(ins):
        into = scratch.at[pl.ds(pl.multiple_of((group ^ other) * size, 16), size)]
        copies.append(pltpu.make_async_copy(in_ref.at[pl.ds(0, size)], into, in_sems.at[other]))
    for copy in copies:
        copy.start()
    rows = lat_outs[0].shape[0]
    lat_size = per_owner * 12
    for other, in_ref in enumerate(ins):
        value = in_ref[size : size + lat_size, :].astype(F32)
        lat_scratch[pl.ds((group ^ other) * lat_size, lat_size), :] = value
    value = pltpu.roll(lat_scratch[: units * 12, :], 64, 1)
    lane = lax.broadcasted_iota(jnp.int32, value.shape, 1)
    for width in (32, 16):
        up, down = pltpu.roll(value, width, 1), pltpu.roll(value, LANES - width, 1)
        value = jnp.where(lane & width == 0, down, up)
    lat_scratch[: units * 12, :] = value
    starts = [band_start(bands, group, source ^ other, owners) for other in range(owners)]
    for copy in copies:
        copy.wait()
    copies = []
    into = [(act_outs[0], 0), (lat_outs[1], 0), (act_outs[1], 0), (act_outs[1], 1)]
    into += [(out, 0) for out in act_outs[2:]]
    length = act_capacity * tiles
    for other, (out_ref, place) in enumerate(into):
        unit = first_unit(starts[other], 1, source, owners, units, act_capacity)
        rows_in = pl.ds(pl.multiple_of(unit * tiles, 16), length)
        rows_out = pl.ds(place * length, length)
        copies.append(
            pltpu.make_async_copy(scratch.at[rows_in], out_ref.at[rows_out], sems.at[other])
        )
    for copy in copies:
        copy.start()
    for other, out_ref in enumerate(lat_outs):
        unit = first_unit(starts[other], 2, source, owners, units, lat_capacity)
        value = lat_scratch[pl.ds(unit * 12, rows), :].astype(BF16)
        out_ref[pl.ds(length if other == 1 else 0, rows), :] = value
    for copy in copies:
        copy.wait()


def shift_columns(sums, width):
    rows = sums.shape[0]
    col = lax.rem(lax.broadcasted_iota(jnp.int32, (rows, width), 0), COLS)
    left = pltpu.roll(sums[:, :width], 1, 0)
    right = pltpu.roll(sums[:, 2 * width :], rows - 1, 0)
    total = sums[:, width : 2 * width] + jnp.where(col > 0, left, 0.0)
    return total + jnp.where(col < COLS - 1, right, 0.0)


def widen_weights(mid_ref, out_ref, mark, sems):
    channels = mid_ref.shape[1]
    mark[...] = jnp.zeros(mark.shape, F32)
    copies = []
    for tap in range(27):
        into = out_ref.at[
            pl.ds(tap // 3 * channels, channels), pl.ds(tap % 3 * channels, channels)
        ]
        copies.append(pltpu.make_async_copy(mid_ref.at[tap], into, sems.at[tap]))
    for copy in copies:
        copy.start()
    for copy in copies:
        copy.wait()


def new_frames(
    bands, win_ref, gain_ref, weights, *refs,
    owners, units, capacity, height, block, band_max, channels, cache_rows,
):
    group = lax.axis_index("seq")
    owner = lax.axis_index("dec")
    lat_refs, refs = refs[:owners], refs[owners:]
    out_ref, part_ref, table, xs, windows_a, windows_b, first_a, first_b = refs[:8]
    act_a, act_b, late, out_sems = refs[8:]
    live = bands[group, owner]
    start = band_start(bands, group, owner, owners)
    edge = lax.rem(height - lax.rem(start - 1 + height, height), height)
    blocks = band_max // block
    size = F * COLS
    per_source = lat_refs[0].shape[0]
    table[...] = jnp.zeros(table.shape, BF16)
    for time_tap in range(3):
        for row_tap in range(3):
            for col_tap in range(3):
                into = row_tap * 2 * LANES + (0, 64, LANES)[time_tap]
                into += ((0, 112, 96), (0, -16, -32), (0, 112, 96))[time_tap][col_tap]
                table[pl.ds(into, 16), :] = win_ref[time_tap * 9 + row_tap * 3 + col_tap]
    for other, lat_ref in enumerate(lat_refs):
        from_row = lat_ref.shape[0] - per_source if other != 1 else cache_rows
        value = lat_ref[pl.ds(from_row, per_source), :].astype(F32)
        rows = pl.ds(pl.multiple_of((owner ^ other) * per_source, 8), per_source)
        xs[0, rows, :] = value
        xs[1, rows, :] = pltpu.roll(value, 64, 1)
    window_zero, act_zero = block + 4, block + 2
    for windows in (windows_a, windows_b):
        windows[window_zero] = jnp.zeros(windows.shape[1:], BF16)
    for act in (act_a, act_b):
        act[act_zero] = jnp.zeros((F, COLS, channels), BF16)
    half_gain = 0.5 * gain_ref[...]

    def clip_edges(at):
        is_first = (at == edge) | (at == edge + height)
        is_last = (at == edge - 1) | (at == edge - 1 + height)
        return is_first, is_last

    def fill(row, windows, into):
        lane = lax.broadcasted_iota(jnp.int32, (8, LANES), 1)
        col = lax.broadcasted_iota(jnp.int32, (8, LANES), 0)
        low = (lane < 16) | (lane >= 96)
        left_end = (col == 0) & ((lane & 63) < 16)
        right_end = (col == 7) & ((lane & 63) >= 32) & ((lane & 63) < 48)
        stack_row = jnp.clip(start - 2 + row, 0, units * owners - 1)
        source = lax.rem(stack_row, owners)
        unit = first_unit(start, 2, source, owners, units, capacity)
        slot = jnp.clip(lax.div(stack_row, owners) - unit, 0, capacity - 1)
        base = source * per_source + slot * 12
        rolled = [{}, {}]
        for frame in range(CT + F):
            for half in range(2):
                at_row = pl.ds(base + half * (CT + F) + frame, 1)
                for turn in range(2):
                    if turn == 1 and not 1 <= frame <= F:
                        continue
                    value = jnp.broadcast_to(xs[turn, at_row, :], (8, LANES))
                    rolled[turn][half, frame] = pltpu.roll(value, 0, 1, stride=16, stride_axis=0)
        for frame in range(F):
            pair = [
                jnp.where(low, rolled[0][half, frame], rolled[1][half, frame + 1])
                for half in range(2)
            ]
            last = [rolled[0][half, frame + 2] for half in range(2)]
            for lanes, (left, right) in enumerate((pair, last)):
                near = jnp.where(left_end, 0.0, jnp.where(right_end, right, left))
                far = jnp.where(right_end, 0.0, jnp.where(left_end, left, right))
                windows[
                    into,
                    frame * COLS : (frame + 1) * COLS,
                    lanes * LANES : (lanes + 1) * LANES,
                ] = jnp.concatenate([near, far], axis=0).astype(BF16)

    def fill_block(row, count, windows):
        for at in range(count + 2):
            fill(row + at, windows, at)

    def convolve_first(row, count, windows):
        pieces = [[], [], []]
        for at in range(count):
            is_first, is_last = clip_edges(row + at)
            pieces[0].append(windows[jnp.where(is_first, window_zero, at)])
            pieces[1].append(windows[at + 1])
            pieces[2].append(windows[jnp.where(is_last, window_zero, at + 2)])
        slab = jnp.concatenate([jnp.concatenate(part, axis=0) for part in pieces], axis=1)
        return jnp.dot(slab, table[...], preferred_element_type=F32)

    def activate(sums, count, into, first, act):
        first[into * size : (into + count) * size, :] = sums
        for at in range(count):
            value = sums[at * size : (at + 1) * size]
            mean_square = jnp.mean(value * value, axis=-1, keepdims=True)
            half = value * lax.rsqrt(mean_square + EPSILON) * half_gain
            value = half + half * jnp.tanh(half)
            act[into + at] = value.astype(BF16).reshape(F, COLS, channels)

    def copy_out(number):
        rows = pl.ds(number * block, block)
        return pltpu.make_async_copy(
            late.at[rows], out_ref.at[rows, pl.ds(2, 2)], out_sems.at[number]
        )

    def convolve(number, first, act):
        begin = number * block
        source_rows = [[], [], []]
        for row in range(block):
            is_first, is_last = clip_edges(begin + row + 1)
            source_rows[0].append(jnp.where(is_first, act_zero, row))
            source_rows[1].append(row + 1)
            source_rows[2].append(jnp.where(is_last, act_zero, row + 2))

        def finish(frames, weight_from, frame_from, count):
            pieces = []
            for frame in frames:
                for row_tap in range(3):
                    parts = [
                        act[at, frame : frame + count].reshape(count * COLS, channels)
                        for at in source_rows[row_tap]
                    ]
                    pieces.append(jnp.concatenate(parts, axis=0))
            slab = jnp.concatenate(pieces, axis=1)
            sums = jnp.dot(slab, weights[weight_from:, :], preferred_element_type=F32)
            total = shift_columns(sums, channels)
            parts = []
            for row in range(block):
                at = (row + 1) * size + frame_from * COLS
                parts.append(first[at : at + count * COLS, :])
            return total + jnp.concatenate(parts, axis=0)

        taps = 3 * channels
        rows = pl.ds(begin, block)
        value = finish([0, 1, 2], 0, 2, 2)
        at_row = lax.broadcasted_iota(jnp.int32, value.shape, 0) // (2 * COLS)
        value = jnp.where(at_row < live - begin, value, 0.0)
        late[rows] = value.astype(BF16).reshape(block, 2, COLS, channels)
        part_ref[rows, 1] = finish([0, 1], taps, 1, 1).reshape(block, COLS, channels)
        part_ref[rows, 0] = finish([0], 2 * taps, 0, 1).reshape(block, COLS, channels)

    def step(number, windows, first, act, next_windows, next_first, next_act):
        sums = convolve_first((number + 1) * block + 2, block, windows)
        for row in range(2):
            next_act[row] = act[block + row]
        next_first[: 2 * size, :] = first[block * size :, :]
        activate(sums, block, 2, next_first, next_act)
        convolve(number, first, act)
        fill_block((number + 2) * block + 2, block, next_windows)
        copy_out(number).start()

    fill_block(0, block + 2, windows_b)
    activate(convolve_first(0, block + 2, windows_b), block + 2, 0, first_a, act_a)
    fill_block(block + 2, block, windows_a)
    used = lax.div(live + block - 1, block)

    def two_steps(pair, carry):
        step(2 * pair, windows_a, first_a, act_a, windows_b, first_b, act_b)

        @pl.when(2 * pair + 1 < used)
        def _():
            step(2 * pair + 1, windows_b, first_b, act_b, windows_a, first_a, act_a)

        return carry

    lax.fori_loop(0, lax.div(used + 1, 2), two_steps, 0)

    def clear(number, carry):
        late[pl.ds(number * block, block)] = jnp.zeros((block, 2, COLS, channels), BF16)
        copy_out(number).start()
        return carry

    lax.fori_loop(used, blocks, clear, 0)
    for number in range(blocks):
        copy_out(number).wait()


def cached_frames(
    bands, part_ref, weights, late_ref, *refs,
    owners, units, capacity, height, block, band_max, channels,
):
    del late_ref
    parts, (out_ref, cache, early, out_sems, cache_sems) = refs[:owners], refs[owners:]
    group = lax.axis_index("seq")
    owner = lax.axis_index("dec")
    live = bands[group, owner]
    start = band_start(bands, group, owner, owners)
    depth = channels // LANES
    blocks = band_max // block
    edge = lax.rem(height - lax.rem(start - 1 + height, height), height)

    def slot_of(at):
        row = jnp.clip(start - 1 + at, 0, units * owners - 1)
        source = lax.rem(row, owners)
        unit = first_unit(start, 1, source, owners, units, capacity)
        return source * capacity + jnp.clip(lax.div(row, owners) - unit, 0, capacity - 1)

    def copy_out(number):
        rows = pl.ds(number * block, block)
        return pltpu.make_async_copy(
            early.at[rows], out_ref.at[rows, pl.ds(0, 2)], out_sems.at[number]
        )

    copies = []
    for other, part in enumerate(parts):
        into = cache.at[pl.ds((owner ^ other) * capacity, capacity)]
        arrived = part.at[pl.ds(0, capacity)]
        copies.append(pltpu.make_async_copy(arrived, into, cache_sems.at[other]))
    for copy in copies:
        copy.start()
    slots = owners * capacity
    cache[slots] = jnp.zeros(cache.shape[1:], BF16)
    for copy in copies:
        copy.wait()
    used = lax.div(live + block - 1, block)

    def convolve(number, carry):
        begin = number * block
        source_rows = [[], [], []]
        for row in range(block):
            at = begin + row + 1
            is_first = (at == edge) | (at == edge + height)
            is_last = (at == edge - 1) | (at == edge - 1 + height)
            source_rows[0].append(jnp.where(is_first, slots, slot_of(at - 1)))
            source_rows[1].append(slot_of(at))
            source_rows[2].append(jnp.where(is_last, slots, slot_of(at + 1)))

        def slab(frames):
            pieces = []
            for frame in frames:
                for row_tap in range(3):
                    for part in range(depth):
                        tile = pl.ds((frame * depth + part) * COLS, COLS)
                        values = [cache[at, tile, :] for at in source_rows[row_tap]]
                        pieces.append(jnp.concatenate(values, axis=0))
            return jnp.concatenate(pieces, axis=1)

        at_row = lax.broadcasted_iota(jnp.int32, (block * COLS, channels), 0) // COLS
        taps = 3 * channels
        rows = pl.ds(begin, block)
        for frame, frames in ((0, (0, 1)), (1, (1,))):
            sums = jnp.dot(
                slab(frames), weights[: len(frames) * taps, :], preferred_element_type=F32
            )
            total = shift_columns(sums, channels) + part_ref[rows, frame].reshape(
                block * COLS, channels
            )
            total = jnp.where(at_row < live - begin, total, 0.0)
            early[rows, frame] = total.astype(BF16).reshape(block, COLS, channels)
        copy_out(number).start()
        return carry

    lax.fori_loop(0, used, convolve, 0)

    def clear(number, carry):
        early[pl.ds(number * block, block)] = jnp.zeros((block, 2, COLS, channels), BF16)
        copy_out(number).start()
        return carry

    lax.fori_loop(used, blocks, clear, 0)
    for number in range(blocks):
        copy_out(number).wait()


def params(mebibytes, **extra):
    return pltpu.CompilerParams(vmem_limit_bytes=mebibytes * 1024 * 1024, **extra)


def shards(latents, cache_lat, cache_act, w_in, w_mid, norm_gain, clip_group, band_rows):
    groups = lax.axis_size("seq")
    owners = lax.axis_size("dec")
    clips = latents.shape[1]
    per_owner = latents.shape[2]
    channels = w_mid.shape[2]
    units = groups * per_owner
    height = per_owner * owners
    stack_rows = groups * height
    band_max = 2 * stack_rows // owners
    act_capacity = (band_max + 2 + owners - 1) // owners
    block = next(size for size in (16, 8) if band_max % size == 0)
    any_space = pl.BlockSpec(memory_space=pl.ANY)
    in_vmem = pl.BlockSpec(memory_space=pltpu.VMEM)
    in_hbm = pl.BlockSpec(memory_space=pltpu.HBM)

    def rows_first(array):
        return jnp.transpose(array[0, :, :, 0, :], (1, 0, 2))

    lat, old, act = rows_first(latents), rows_first(cache_lat), rows_first(cache_act)
    tiles = act.shape[2] // LANES
    lat_rows = (per_owner * 12 + 15) // 16 * 16
    per_step = 3
    packed = pl.pallas_call(
        functools.partial(
            pack_clips, per_owner=per_owner, per_step=per_step, clips=clips
        ),
        grid_spec=pltpu.PrefetchScalarGridSpec(
            num_scalar_prefetch=1,
            grid=(),
            in_specs=[in_hbm, in_hbm, in_hbm],
            out_specs=[in_vmem] * clips,
            scratch_shapes=[
                pltpu.VMEM(lat.shape, BF16),
                pltpu.VMEM(old.shape, BF16),
                pltpu.VMEM(act.shape, BF16),
                pltpu.VMEM((clips * lat_rows, LANES), F32),
                pltpu.VMEM((2, clips * per_step * tiles, LANES), F32),
                pltpu.SemaphoreType.DMA((2 + per_owner // per_step,)),
            ],
        ),
        out_shape=[jax.ShapeDtypeStruct((per_owner * tiles + lat_rows, LANES), BF16)] * clips,
        compiler_params=params(56),
        name="pack_clips",
    )(clip_group, lat, old, act)

    def trade(parts, axis):
        count = lax.axis_size(axis)
        return [parts[0]] + [
            lax.ppermute(part, axis, [(i, i ^ other) for i in range(count)])
            for other, part in enumerate(parts)
            if other
        ]

    traded = trade(packed, "seq")
    wide_mid, mark = pl.pallas_call(
        widen_weights,
        in_specs=[in_hbm],
        out_specs=[in_vmem, in_vmem],
        scratch_shapes=[pltpu.SemaphoreType.DMA((27,))],
        out_shape=[
            jax.ShapeDtypeStruct((9 * channels, 3 * channels), BF16),
            jax.ShapeDtypeStruct((8, LANES), F32),
        ],
        compiler_params=params(16),
        cost_estimate=pl.CostEstimate(
            flops=0, bytes_accessed=4 * 27 * channels * channels, transcendentals=0
        ),
        name="widen_weights",
    )(w_mid)
    lat_capacity = (band_max + 4 + owners - 1) // owners
    slice_rows = (lat_capacity * 12 + 15) // 16 * 16
    slice_both = (act_capacity * tiles + slice_rows + tiles - 1) // tiles * tiles
    slice_act = jax.ShapeDtypeStruct((act_capacity * tiles, LANES), BF16)
    slice_two = jax.ShapeDtypeStruct((2 * act_capacity * tiles, LANES), BF16)
    sliced = pl.pallas_call(
        functools.partial(
            slice_bands, owners=owners, units=units, lat_capacity=lat_capacity,
            act_capacity=act_capacity, per_owner=per_owner, tiles=tiles, groups=groups,
        ),
        grid_spec=pltpu.PrefetchScalarGridSpec(
            num_scalar_prefetch=1,
            grid=(),
            in_specs=[in_vmem] * (1 + clips),
            out_specs=[in_vmem] * (2 * owners - 2),
            scratch_shapes=[
                pltpu.VMEM((units * 12 + slice_rows, LANES), F32),
                pltpu.VMEM((units * tiles, LANES), BF16),
                pltpu.SemaphoreType.DMA((clips,)),
                pltpu.SemaphoreType.DMA((owners,)),
            ],
        ),
        out_shape=[
            jax.ShapeDtypeStruct((slice_both if other == 1 else slice_rows, LANES), BF16)
            for other in range(owners)
        ]
        + [slice_act, slice_two]
        + [slice_act] * (owners - 4),
        compiler_params=params(16),
        name="slice_bands",
    )(band_rows, mark, *traded)
    band_lat, band_act = lax.optimization_barrier(
        (trade(sliced[:owners], "dec"), sliced[owners:])
    )

    def send(part, other):
        return lax.ppermute(part, "dec", [(i, i ^ other) for i in range(owners)])

    own, *band_act = band_act
    far = [send(part, other) for other, part in enumerate(band_act[1:], 4)]
    two = send(band_act[0], 2)

    late, part = pl.pallas_call(
        functools.partial(
            new_frames, owners=owners, units=units, capacity=lat_capacity, height=height,
            block=block, band_max=band_max, channels=channels, cache_rows=act_capacity * tiles,
        ),
        grid_spec=pltpu.PrefetchScalarGridSpec(
            num_scalar_prefetch=1,
            grid=(),
            in_specs=[in_vmem] * (3 + owners),
            out_specs=[in_hbm, in_vmem],
            scratch_shapes=[
                pltpu.VMEM((6 * LANES, channels), BF16),
                pltpu.VMEM((2, owners * slice_rows, LANES), F32),
                pltpu.VMEM((block + 5, F * COLS, 2 * LANES), BF16),
                pltpu.VMEM((block + 5, F * COLS, 2 * LANES), BF16),
                pltpu.VMEM(((block + 2) * F * COLS, channels), F32),
                pltpu.VMEM(((block + 2) * F * COLS, channels), F32),
                pltpu.VMEM((block + 3, F, COLS, channels), BF16),
                pltpu.VMEM((block + 3, F, COLS, channels), BF16),
                pltpu.VMEM((band_max, 2, COLS, channels), BF16),
                pltpu.SemaphoreType.DMA((band_max // block,)),
            ],
        ),
        out_shape=[
            jax.ShapeDtypeStruct((band_max, F, COLS, channels), BF16),
            jax.ShapeDtypeStruct((band_max, 2, COLS, channels), F32),
        ],
        compiler_params=params(36),
        cost_estimate=pl.CostEstimate(
            flops=2 * band_max * 9 * COLS * 9 * channels * channels,
            bytes_accessed=16 * 1024 * 1024,
            transcendentals=0,
        ),
        name="new_frames",
    )(band_rows, w_in, norm_gain.reshape(1, channels), wide_mid, *band_lat)

    slots = owners * act_capacity
    two, part = lax.optimization_barrier((two, part))
    handed = send(two[act_capacity * tiles :], 1)
    band_act = [rows.reshape(-1, tiles, LANES) for rows in (own, band_lat[1], two, handed, *far)]
    decoded = pl.pallas_call(
        functools.partial(
            cached_frames, owners=owners, units=units, capacity=act_capacity, height=height,
            block=block, band_max=band_max, channels=channels,
        ),
        grid_spec=pltpu.PrefetchScalarGridSpec(
            num_scalar_prefetch=1,
            grid=(),
            in_specs=[in_vmem, in_vmem, in_hbm] + [any_space] * owners,
            out_specs=in_hbm,
            scratch_shapes=[
                pltpu.VMEM((slots + 1, tiles, LANES), BF16),
                pltpu.VMEM((band_max, 2, COLS, channels), BF16),
                pltpu.SemaphoreType.DMA((band_max // block,)),
                pltpu.SemaphoreType.DMA((owners,)),
            ],
        ),
        out_shape=jax.ShapeDtypeStruct((band_max, F, COLS, channels), BF16),
        input_output_aliases={3: 0},
        compiler_params=params(24),
        cost_estimate=pl.CostEstimate(
            flops=2 * band_max * 3 * COLS * 9 * channels * channels,
            bytes_accessed=16 * 1024 * 1024,
            transcendentals=0,
        ),
        name="cached_frames",
    )(band_rows, part, wide_mid, late, *band_act)
    return decoded.reshape((1, 1) + decoded.shape)


def solution(mesh):
    placed = (
        P("seq", None, None, "dec", None),
        P("seq", None, None, "dec", None),
        P("seq", None, None, "dec", None),
        P(),
        P(),
        P(),
        P(),
        P(),
    )
    return jax.shard_map(
        shards,
        mesh=mesh,
        in_specs=placed,
        out_specs=P("seq", "dec", None, None, None, None),
        check_vma=False,
    )
```

profile of v0, /device:TPU:11, one launch (start us, length us, event | category | flops | bytes accessed | tf_op | source)
XLA Modules:
  0.0 119.9 jit_solution(18203478548626654962)
XLA Ops:
  0.0 4.5 %pack_clips.1 = (bf16[1296,128]{1,0:T(8,128)(2,1)}, bf16[1296,128]{1,0:T(8,128)(2,1)}, bf16[1296,128]{1,0:T(8,128)(2,1)}, bf16[1296,128]{1,0:T(8,128)(2,1)}) custom-call(s32[4,4]{1,0:T(4,128)} %groups_ref.1, bf16[12,4,1024]{2,1,0:T(4,128)(2,1)} %bitcast.27, bf16[12,4,512]{2,1,0:T(4,128)(2,1)} %bitcast.28, bf16[12,4,12288]{2,1,0:T(4,128)(2,1)} %bitcast.26), custom_call_target="tpu_custom_call" | custom-call | tf_op jit(solution)/shard_map/pack_clips/pallas_call | solution.py:454
  4.8 1.2 %collective-permute-start.1 = (bf16[1296,128]{1,0:T(8,128)(2,1)}, bf16[1296,128]{1,0:T(8,128)(2,1)S(1)}, u32[]{:S(2)}, u32[]{:S(2)}) collective-permute-start(bf16[1296,128]{1,0:T(8,128)(2,1)} %get-tuple-element.46), channel_id=1, source_target_pairs={{0,16},{8,24},{16,0},{24,8},{1,17},{9,25},{17,1},{25,9},{2,18},{10... | collective-permute-start | bytes 995336 | tf_op jit(solution)/shard_map/ppermute | solution.py:480
  6.1 1.2 collective-permute-start.2
  7.2 3.3 %copy-done = bf16[27,384,384]{2,1,0:T(8,128)(2,1)S(1)} copy-done((bf16[27,384,384]{2,1,0:T(8,128)(2,1)S(1)}, bf16[27,384,384]{2,1,0:T(8,128)(2,1)}, u32[]{:S(2)}) %copy-start) | copy-done | bytes 7962648
  10.5 1.1 widen_weights.1
  11.6 1.8 %collective-permute-done.refs_1_ = bf16[1296,128]{1,0:T(8,128)(2,1)S(1)} collective-permute-done((bf16[1296,128]{1,0:T(8,128)(2,1)}, bf16[1296,128]{1,0:T(8,128)(2,1)S(1)}, u32[]{:S(2)}, u32[]{:S(2)}) %collective-permute-start) | collective-permute-done | bytes 331808 | tf_op jit(solution)/shard_map/ppermute | solution.py:480
  13.5 8.1 %collective-permute-done.2.refs_3_ = bf16[1296,128]{1,0:T(8,128)(2,1)S(1)} collective-permute-done((bf16[1296,128]{1,0:T(8,128)(2,1)}, bf16[1296,128]{1,0:T(8,128)(2,1)S(1)}, u32[]{:S(2)}, u32[]{:S(2)}) %collective-permute-start.2) | collective-permute-done | bytes 331808 | tf_op jit(solution)/shard_map/ppermute | solution.py:480
  21.5 2.3 %slice_bands.1 = (bf16[160,128]{1,0:T(8,128)(2,1)S(1)}, bf16[1440,128]{1,0:T(8,128)(2,1)S(1)}, bf16[160,128]{1,0:T(8,128)(2,1)S(1)}, bf16[160,128]{1,0:T(8,128)(...) custom-call(s32[4,8]{1,0:T(4,128)S(1)} %copy-done.2, ...), custom_call_target="tpu_custom_call" | custom-call | tf_op jit(solution)/shard_map/slice_bands/pallas_call | solution.py:506
  23.8 1.6 %collective-permute-start.3 = (bf16[1440,128]{1,0:T(8,128)(2,1)S(1)}, bf16[1440,128]{1,0:T(8,128)(2,1)S(1)}, u32[]{:S(2)}, u32[]{:S(2)}) collective-permute-start(bf16[1440,128]{1,0:T(8,128)(2,1)S(1)} %get-tuple-element.49), channel_id=1, source_target_pairs={{0,1},{1,0},{2,3},{3,2},{4,5},{5,4},{6,7},{7,6},{8,9},{9,8},{10,11... | collective-permute-start | bytes 1105928 | tf_op jit(solution)/shard_map/ppermute | solution.py:480
  25.6 1.5 %collective-permute-start.5 = (bf16[160,128]{1,0:T(8,128)(2,1)S(1)}, bf16[160,128]{1,0:T(8,128)(2,1)S(1)}, u32[]{:S(2)}, u32[]{:S(2)}) collective-permute-start(bf16[160,128]{1,0:T(8,128)(2,1)S(1)} %get-tuple-element.51), channel_id=1, source_target_pairs={{0,3},{1,2},{2,1},{3,0},{4,7},{5,6},{6,5},{7,4},{8,11},{9,10},{10,... | collective-permute-start | bytes 122888 | tf_op jit(solution)/shard_map/ppermute | solution.py:480
  27.2 2.3 %collective-permute-start.6 = (bf16[160,128]{1,0:T(8,128)(2,1)S(1)}, bf16[160,128]{1,0:T(8,128)(2,1)S(1)}, u32[]{:S(2)}, u32[]{:S(2)}) collective-permute-start(bf16[160,128]{1,0:T(8,128)(2,1)S(1)} %get-tuple-element.52), channel_id=1, source_target_pairs={{0,4},{1,5},{2,6},{3,7},{4,0},{5,1},{6,2},{7,3},{8,12},{9,13},{10,... | collective-permute-start | bytes 122888 | tf_op jit(solution)/shard_map/ppermute | solution.py:480
  29.9 1.3 %collective-permute-start.8 = (bf16[160,128]{1,0:T(8,128)(2,1)S(1)}, bf16[160,128]{1,0:T(8,128)(2,1)S(1)}, u32[]{:S(2)}, u32[]{:S(2)}) collective-permute-start(bf16[160,128]{1,0:T(8,128)(2,1)S(1)} %get-tuple-element.54), channel_id=1, source_target_pairs={{0,6},{1,7},{2,4},{3,5},{4,2},{5,3},{6,0},{7,1},{8,14},{9,15},{10,... | collective-permute-start | bytes 122888 | tf_op jit(solution)/shard_map/ppermute | solution.py:480
  31.2 0.6 collective-permute-start.9
  31.8 0.5 collective-permute-done.6.refs_4_
  32.3 2.0 %collective-permute-done.7.refs_5_ = bf16[160,128]{1,0:T(8,128)(2,1)S(1)} collective-permute-done((bf16[160,128]{1,0:T(8,128)(2,1)S(1)}, bf16[160,128]{1,0:T(8,128)(2,1)S(1)}, u32[]{:S(2)}, u32[]{:S(2)}) %collective-permute-start.7) | collective-permute-done | bytes 40992 | tf_op jit(solution)/shard_map/ppermute | solution.py:480
  34.3 1.5 %collective-permute-done.8.refs_6_ = bf16[160,128]{1,0:T(8,128)(2,1)S(1)} collective-permute-done((bf16[160,128]{1,0:T(8,128)(2,1)S(1)}, bf16[160,128]{1,0:T(8,128)(2,1)S(1)}, u32[]{:S(2)}, u32[]{:S(2)}) %collective-permute-start.8) | collective-permute-done | bytes 40992 | tf_op jit(solution)/shard_map/ppermute | solution.py:480
  35.8 1.0 collective-permute-done.9.refs_7_
  36.8 1.4 %collective-permute-start.12 = (bf16[1248,128]{1,0:T(8,128)(2,1)S(1)}, bf16[1248,128]{1,0:T(8,128)(2,1)S(1)}, u32[]{:S(2)}, u32[]{:S(2)}) collective-permute-start(bf16[1248,128]{1,0:T(8,128)(2,1)S(1)} %get-tuple-element.77), channel_id=1, source_target_pairs={{0,4},{1,5},{2,6},{3,7},{4,0},{5,1},{6,2},{7,3},{8,12},{9,13},{10,... | collective-permute-start | bytes 958472 | tf_op jit(solution)/shard_map/ppermute | solution.py:537
  38.3 1.6 %collective-permute-start.13 = (bf16[1248,128]{1,0:T(8,128)(2,1)S(1)}, bf16[1248,128]{1,0:T(8,128)(2,1)S(1)}, u32[]{:S(2)}, u32[]{:S(2)}) collective-permute-start(bf16[1248,128]{1,0:T(8,128)(2,1)S(1)} %get-tuple-element.78), channel_id=1, source_target_pairs={{0,5},{1,4},{2,7},{3,6},{4,1},{5,0},{6,3},{7,2},{8,13},{9,12},{10,... | collective-permute-start | bytes 958472 | tf_op jit(solution)/shard_map/ppermute | solution.py:537
  39.8 2.1 %collective-permute-start.14 = (bf16[1248,128]{1,0:T(8,128)(2,1)S(1)}, bf16[1248,128]{1,0:T(8,128)(2,1)S(1)}, u32[]{:S(2)}, u32[]{:S(2)}) collective-permute-start(bf16[1248,128]{1,0:T(8,128)(2,1)S(1)} %get-tuple-element.79), channel_id=1, source_target_pairs={{0,6},{1,7},{2,4},{3,5},{4,2},{5,3},{6,0},{7,1},{8,14},{9,15},{10,... | collective-permute-start | bytes 958472 | tf_op jit(solution)/shard_map/ppermute | solution.py:537
  42.0 2.9 %collective-permute-start.10 = (bf16[2496,128]{1,0:T(8,128)(2,1)S(1)}, bf16[2496,128]{1,0:T(8,128)(2,1)S(1)}, u32[]{:S(2)}, u32[]{:S(2)}) collective-permute-start(bf16[2496,128]{1,0:T(8,128)(2,1)S(1)} %get-tuple-element.62), channel_id=1, source_target_pairs={{0,2},{1,3},{2,0},{3,1},{4,6},{5,7},{6,4},{7,5},{8,10},{9,11},{10,... | collective-permute-start | bytes 1916936 | tf_op jit(solution)/shard_map/ppermute | solution.py:537
  44.9 54.2 %new_frames.1 = (bf16[96,4,16,384]{3,2,1,0:T(8,128)(2,1)}, f32[96,2,16,384]{3,2,1,0:T(8,128)S(1)}) custom-call(s32[4,8]{1,0:T(4,128)S(1)} %copy-done.2, bf16[27,16,384]{2,1,0:T(8,128)(2,1)S(1)} %copy-done.3, f32[1,384]{1,0:T(1,128)S(1)} %reshape.30.gain_ref, bf16[3456,1152]{1,0:T(8,128)(2,1)S(1)} %get-tuple-element.63.weights, ...), custom_call_target="tpu_custom_call" | custom-call | flops 36691771392 | bytes 16777216 | tf_op jit(solution)/shard_map/new_frames/pallas_call | solution.py:543
  99.2 1.6 %collective-permute-done.11 = bf16[1248,128]{1,0:T(8,128)(2,1)S(1)} collective-permute-done((bf16[1248,128]{1,0:T(8,128)(2,1)S(1)}, bf16[1248,128]{1,0:T(8,128)(2,1)S(1)}, u32[]{:S(2)}, u32[]{:S(2)}) %collective-permute-start.11) | collective-permute-done | bytes 319520 | tf_op jit(solution)/shard_map/ppermute | solution.py:537
  100.8 18.9 %cached_frames.1 = bf16[96,4,16,384]{3,2,1,0:T(8,128)(2,1)} custom-call(s32[4,8]{1,0:T(4,128)S(1)} %copy-done.2, f32[96,2,16,384]{3,2,1,0:T(8,128)S(1)} %get-tuple-element.73.part_ref, bf16[3456,1152]{1,0:T(8,128)(2,1)S(1)} %get-tuple-element.63.weights, bf16[96,4,16,384]{3,2,1,0:T(8,128)(2,1)} %get-tuple-element.74.late_ref, ...), custom_call_target="tpu_custom_call", output_to_operand_aliasing={{}: (3, {})} | custom-call | flops 12230590464 | bytes 16777216 | tf_op jit(solution)/shard_map/cached_frames/pallas_call | solution.py:583
  (25 shorter events, 1.0 us)
Async XLA Ops:
  0.0 21.5 %copy-start.2 = (s32[4,8]{1,0:T(4,128)S(1)}, s32[4,8]{1,0:T(4,128)}, u32[]{:S(2)}) copy-start(s32[4,8]{1,0:T(4,128)} %bands.5) | copy-start | bytes 388
  0.0 44.9 %copy-start.3 = (bf16[27,16,384]{2,1,0:T(8,128)(2,1)S(1)}, bf16[27,16,384]{2,1,0:T(8,128)(2,1)}, u32[]{:S(2)}) copy-start(bf16[27,16,384]{2,1,0:T(8,128)(2,1)} %win_ref.1) | copy-start | bytes 995332
  4.5 27.3 %copy-start.4 = (f32[384]{0:T(512)S(1)}, f32[384]{0:T(512)}, u32[]{:S(2)}) copy-start(f32[384]{0:T(512)} %param.13) | copy-start | bytes 4612
  4.5 8.9 %collective-permute-start = (bf16[1296,128]{1,0:T(8,128)(2,1)}, bf16[1296,128]{1,0:T(8,128)(2,1)S(1)}, u32[]{:S(2)}, u32[]{:S(2)}) collective-permute-start(bf16[1296,128]{1,0:T(8,128)(2,1)} %get-tuple-element.45), channel_id=1, source_target_pairs={{0,8},{8,0},{16,24},{24,16},{1,9},{9,1},{17,25},{25,17},{2,10},{10... | collective-permute-start | bytes 995336 | tf_op jit(solution)/shard_map/ppermute | solution.py:480
  4.8 8.6 %collective-permute-start.1 = (bf16[1296,128]{1,0:T(8,128)(2,1)}, bf16[1296,128]{1,0:T(8,128)(2,1)S(1)}, u32[]{:S(2)}, u32[]{:S(2)}) collective-permute-start(bf16[1296,128]{1,0:T(8,128)(2,1)} %get-tuple-element.46), channel_id=1, source_target_pairs={{0,16},{8,24},{16,0},{24,8},{1,17},{9,25},{17,1},{25,9},{2,18},{10... | collective-permute-start | bytes 995336 | tf_op jit(solution)/shard_map/ppermute | solution.py:480
  6.1 15.4 %collective-permute-start.2 = (bf16[1296,128]{1,0:T(8,128)(2,1)}, bf16[1296,128]{1,0:T(8,128)(2,1)S(1)}, u32[]{:S(2)}, u32[]{:S(2)}) collective-permute-start(bf16[1296,128]{1,0:T(8,128)(2,1)} %get-tuple-element.47), channel_id=1, source_target_pairs={{0,24},{8,16},{16,8},{24,0},{1,25},{9,17},{17,9},{25,1},{2,26},{10... | collective-permute-start | bytes 995336 | tf_op jit(solution)/shard_map/ppermute | solution.py:480
  7.2 3.3 %copy-start = (bf16[27,384,384]{2,1,0:T(8,128)(2,1)S(1)}, bf16[27,384,384]{2,1,0:T(8,128)(2,1)}, u32[]{:S(2)}) copy-start(bf16[27,384,384]{2,1,0:T(8,128)(2,1)} %mid_ref.1) | copy-start | bytes 23887876
  10.5 11.0 %copy-start.1 = (bf16[1296,128]{1,0:T(8,128)(2,1)S(1)}, bf16[1296,128]{1,0:T(8,128)(2,1)}, u32[]{:S(2)}) copy-start(bf16[1296,128]{1,0:T(8,128)(2,1)} %get-tuple-element.44.refs_0_) | copy-start | bytes 995332
  23.8 13.0 %collective-permute-start.3 = (bf16[1440,128]{1,0:T(8,128)(2,1)S(1)}, bf16[1440,128]{1,0:T(8,128)(2,1)S(1)}, u32[]{:S(2)}, u32[]{:S(2)}) collective-permute-start(bf16[1440,128]{1,0:T(8,128)(2,1)S(1)} %get-tuple-element.49), channel_id=1, source_target_pairs={{0,1},{1,0},{2,3},{3,2},{4,5},{5,4},{6,7},{7,6},{8,9},{9,8},{10,11... | collective-permute-start | bytes 1105928 | tf_op jit(solution)/shard_map/ppermute | solution.py:480
  25.5 4.4 %collective-permute-start.4 = (bf16[160,128]{1,0:T(8,128)(2,1)S(1)}, bf16[160,128]{1,0:T(8,128)(2,1)S(1)}, u32[]{:S(2)}, u32[]{:S(2)}) collective-permute-start(bf16[160,128]{1,0:T(8,128)(2,1)S(1)} %get-tuple-element.50), channel_id=1, source_target_pairs={{0,2},{1,3},{2,0},{3,1},{4,6},{5,7},{6,4},{7,5},{8,10},{9,11},{10,... | collective-permute-start | bytes 122888 | tf_op jit(solution)/shard_map/ppermute | solution.py:480
  25.6 5.5 %collective-permute-start.5 = (bf16[160,128]{1,0:T(8,128)(2,1)S(1)}, bf16[160,128]{1,0:T(8,128)(2,1)S(1)}, u32[]{:S(2)}, u32[]{:S(2)}) collective-permute-start(bf16[160,128]{1,0:T(8,128)(2,1)S(1)} %get-tuple-element.51), channel_id=1, source_target_pairs={{0,3},{1,2},{2,1},{3,0},{4,7},{5,6},{6,5},{7,4},{8,11},{9,10},{10,... | collective-permute-start | bytes 122888 | tf_op jit(solution)/shard_map/ppermute | solution.py:480
  27.2 5.1 %collective-permute-start.6 = (bf16[160,128]{1,0:T(8,128)(2,1)S(1)}, bf16[160,128]{1,0:T(8,128)(2,1)S(1)}, u32[]{:S(2)}, u32[]{:S(2)}) collective-permute-start(bf16[160,128]{1,0:T(8,128)(2,1)S(1)} %get-tuple-element.52), channel_id=1, source_target_pairs={{0,4},{1,5},{2,6},{3,7},{4,0},{5,1},{6,2},{7,3},{8,12},{9,13},{10,... | collective-permute-start | bytes 122888 | tf_op jit(solution)/shard_map/ppermute | solution.py:480
  29.5 4.9 %collective-permute-start.7 = (bf16[160,128]{1,0:T(8,128)(2,1)S(1)}, bf16[160,128]{1,0:T(8,128)(2,1)S(1)}, u32[]{:S(2)}, u32[]{:S(2)}) collective-permute-start(bf16[160,128]{1,0:T(8,128)(2,1)S(1)} %get-tuple-element.53), channel_id=1, source_target_pairs={{0,5},{1,4},{2,7},{3,6},{4,1},{5,0},{6,3},{7,2},{8,13},{9,12},{10,... | collective-permute-start | bytes 122888 | tf_op jit(solution)/shard_map/ppermute | solution.py:480
  29.9 5.9 %collective-permute-start.8 = (bf16[160,128]{1,0:T(8,128)(2,1)S(1)}, bf16[160,128]{1,0:T(8,128)(2,1)S(1)}, u32[]{:S(2)}, u32[]{:S(2)}) collective-permute-start(bf16[160,128]{1,0:T(8,128)(2,1)S(1)} %get-tuple-element.54), channel_id=1, source_target_pairs={{0,6},{1,7},{2,4},{3,5},{4,2},{5,3},{6,0},{7,1},{8,14},{9,15},{10,... | collective-permute-start | bytes 122888 | tf_op jit(solution)/shard_map/ppermute | solution.py:480
  31.2 5.7 %collective-permute-start.9 = (bf16[160,128]{1,0:T(8,128)(2,1)S(1)}, bf16[160,128]{1,0:T(8,128)(2,1)S(1)}, u32[]{:S(2)}, u32[]{:S(2)}) collective-permute-start(bf16[160,128]{1,0:T(8,128)(2,1)S(1)} %get-tuple-element.55), channel_id=1, source_target_pairs={{0,7},{1,6},{2,5},{3,4},{4,3},{5,2},{6,1},{7,0},{8,15},{9,14},{10,... | collective-permute-start | bytes 122888 | tf_op jit(solution)/shard_map/ppermute | solution.py:480
  36.8 62.3 %collective-permute-start.12 = (bf16[1248,128]{1,0:T(8,128)(2,1)S(1)}, bf16[1248,128]{1,0:T(8,128)(2,1)S(1)}, u32[]{:S(2)}, u32[]{:S(2)}) collective-permute-start(bf16[1248,128]{1,0:T(8,128)(2,1)S(1)} %get-tuple-element.77), channel_id=1, source_target_pairs={{0,4},{1,5},{2,6},{3,7},{4,0},{5,1},{6,2},{7,3},{8,12},{9,13},{10,... | collective-permute-start | bytes 958472 | tf_op jit(solution)/shard_map/ppermute | solution.py:537
  38.3 60.9 %collective-permute-start.13 = (bf16[1248,128]{1,0:T(8,128)(2,1)S(1)}, bf16[1248,128]{1,0:T(8,128)(2,1)S(1)}, u32[]{:S(2)}, u32[]{:S(2)}) collective-permute-start(bf16[1248,128]{1,0:T(8,128)(2,1)S(1)} %get-tuple-element.78), channel_id=1, source_target_pairs={{0,5},{1,4},{2,7},{3,6},{4,1},{5,0},{6,3},{7,2},{8,13},{9,12},{10,... | collective-permute-start | bytes 958472 | tf_op jit(solution)/shard_map/ppermute | solution.py:537
  39.8 59.4 %collective-permute-start.14 = (bf16[1248,128]{1,0:T(8,128)(2,1)S(1)}, bf16[1248,128]{1,0:T(8,128)(2,1)S(1)}, u32[]{:S(2)}, u32[]{:S(2)}) collective-permute-start(bf16[1248,128]{1,0:T(8,128)(2,1)S(1)} %get-tuple-element.79), channel_id=1, source_target_pairs={{0,6},{1,7},{2,4},{3,5},{4,2},{5,3},{6,0},{7,1},{8,14},{9,15},{10,... | collective-permute-start | bytes 958472 | tf_op jit(solution)/shard_map/ppermute | solution.py:537
  42.0 57.2 %collective-permute-start.15 = (bf16[1248,128]{1,0:T(8,128)(2,1)S(1)}, bf16[1248,128]{1,0:T(8,128)(2,1)S(1)}, u32[]{:S(2)}, u32[]{:S(2)}) collective-permute-start(bf16[1248,128]{1,0:T(8,128)(2,1)S(1)} %get-tuple-element.80), channel_id=1, source_target_pairs={{0,7},{1,6},{2,5},{3,4},{4,3},{5,2},{6,1},{7,0},{8,15},{9,14},{10,... | collective-permute-start | bytes 958472 | tf_op jit(solution)/shard_map/ppermute | solution.py:537
  42.0 57.1 %collective-permute-start.10 = (bf16[2496,128]{1,0:T(8,128)(2,1)S(1)}, bf16[2496,128]{1,0:T(8,128)(2,1)S(1)}, u32[]{:S(2)}, u32[]{:S(2)}) collective-permute-start(bf16[2496,128]{1,0:T(8,128)(2,1)S(1)} %get-tuple-element.62), channel_id=1, source_target_pairs={{0,2},{1,3},{2,0},{3,1},{4,6},{5,7},{6,4},{7,5},{8,10},{9,11},{10,... | collective-permute-start | bytes 1916936 | tf_op jit(solution)/shard_map/ppermute | solution.py:537
  99.1 1.7 %collective-permute-start.11 = (bf16[1248,128]{1,0:T(8,128)(2,1)S(1)}, bf16[1248,128]{1,0:T(8,128)(2,1)S(1)}, u32[]{:S(2)}, u32[]{:S(2)}) collective-permute-start(bf16[1248,128]{1,0:T(8,128)(2,1)S(1)} %slice.3), channel_id=1, source_target_pairs={{0,1},{1,0},{2,3},{3,2},{4,5},{5,4},{6,7},{7,6},{8,9},{9,8},{10,11... | collective-permute-start | bytes 958472 | tf_op jit(solution)/shard_map/ppermute | solution.py:537
where the time goes:
time: 120 us
  Pallas kernels  81 us (68%)
  starting transfers between devices  18.8 us (16%)
  waiting for transfers between devices  16.5 us (14%)
  local copies, waits for them, and re-layouts  3.3 us (3%)
    pallas_call x1, Pallas kernels, shards(): pl.pallas_call(functools.partial(new_frames, owners=owners, units=units,...  54.2 us
    pallas_call x1, Pallas kernels, shards(): pl.pallas_call(functools.partial(cached_frames, owners=owners, units=unit...  18.9 us
    ppermute x10, waiting for transfers between devices, trade(): lax.ppermute(part, axis, [(i, i ^ other) for i in range(count)])  14.9 us
    ppermute x10, starting transfers between devices, trade(): lax.ppermute(part, axis, [(i, i ^ other) for i in range(count)])  10.7 us
    ppermute x6, starting transfers between devices, send(): return lax.ppermute(part, 'dec', [(i, i ^ other) for i in range(owners)])  8.11 us
    pallas_call x1, Pallas kernels, shards(): pl.pallas_call(functools.partial(pack_clips, per_owner=per_owner, per_ste...  4.5 us
    unnamed x10, local copies, waits for them, and re-layouts  3.28 us
  transfers between devices with their start and end apart: 16, of which 7 were waited for; matrix products, arithmetic and copies ran while one was open for 0% of the time, Pallas kernels for 46%

commit v1 on v0

--- a/solution.py
+++ b/solution.py
@@ -91,7 +91,7 @@
 def slice_bands(
     bands, _, *refs, owners, units, lat_capacity, act_capacity, per_owner, tiles, groups
 ):
-    ins, lat_outs, act_outs = refs[:groups], refs[groups : groups + owners], refs[groups + owners : -4]
+    ins, lat_out, act_outs = refs[:groups], refs[groups], refs[groups + 1 : -4]
     lat_scratch, scratch, in_sems, sems = refs[-4:]
     group = lax.axis_index("seq")
     source = lax.axis_index("dec")
@@ -102,7 +102,7 @@
         copies.append(pltpu.make_async_copy(in_ref.at[pl.ds(0, size)], into, in_sems.at[other]))
     for copy in copies:
         copy.start()
-    rows = lat_outs[0].shape[0]
+    rows = lat_out.shape[1]
     lat_size = per_owner * 12
     for other, in_ref in enumerate(ins):
         value = in_ref[size : size + lat_size, :].astype(F32)
@@ -117,8 +117,8 @@
     for copy in copies:
         copy.wait()
     copies = []
-    into = [(act_outs[0], 0), (lat_outs[1], 0), (act_outs[1], 0), (act_outs[1], 1)]
-    into += [(out, 0) for out in act_outs[2:]]
+    into = [(act_outs[0], 0), (act_outs[1], 0), (act_outs[2], 0), (act_outs[2], 1)]
+    into += [(out, 0) for out in act_outs[3:]]
     length = act_capacity * tiles
     for other, (out_ref, place) in enumerate(into):
         unit = first_unit(starts[other], 1, source, owners, units, act_capacity)
@@ -129,10 +129,9 @@
         )
     for copy in copies:
         copy.start()
-    for other, out_ref in enumerate(lat_outs):
+    for other in range(owners):
         unit = first_unit(starts[other], 2, source, owners, units, lat_capacity)
-        value = lat_scratch[pl.ds(unit * 12, rows), :].astype(BF16)
-        out_ref[pl.ds(length if other == 1 else 0, rows), :] = value
+        lat_out[source ^ other] = lat_scratch[pl.ds(unit * 12, rows), :].astype(BF16)
     for copy in copies:
         copy.wait()
 
@@ -146,36 +145,19 @@
     return total + jnp.where(col < COLS - 1, right, 0.0)
 
 
-def widen_weights(mid_ref, out_ref, mark, sems):
+def widen_weights(mid_ref, win_ref, out_ref, table, wide, sems, out_sems):
     channels = mid_ref.shape[1]
-    mark[...] = jnp.zeros(mark.shape, F32)
-    copies = []
+    copies, stores = [], []
     for tap in range(27):
-        into = out_ref.at[
-            pl.ds(tap // 3 * channels, channels), pl.ds(tap % 3 * channels, channels)
-        ]
+        rows = pl.ds(tap // 3 * channels, channels)
+        into = wide.at[rows, pl.ds(tap % 3 * channels, channels)]
         copies.append(pltpu.make_async_copy(mid_ref.at[tap], into, sems.at[tap]))
+        if tap % 3 == 2:
+            stores.append(
+                pltpu.make_async_copy(wide.at[rows], out_ref.at[rows], out_sems.at[tap // 3])
+            )
     for copy in copies:
         copy.start()
-    for copy in copies:
-        copy.wait()
-
-
-def new_frames(
-    bands, win_ref, gain_ref, weights, *refs,
-    owners, units, capacity, height, block, band_max, channels, cache_rows,
-):
-    group = lax.axis_index("seq")
-    owner = lax.axis_index("dec")
-    lat_refs, refs = refs[:owners], refs[owners:]
-    out_ref, part_ref, table, xs, windows_a, windows_b, first_a, first_b = refs[:8]
-    act_a, act_b, late, out_sems = refs[8:]
-    live = bands[group, owner]
-    start = band_start(bands, group, owner, owners)
-    edge = lax.rem(height - lax.rem(start - 1 + height, height), height)
-    blocks = band_max // block
-    size = F * COLS
-    per_source = lat_refs[0].shape[0]
     table[...] = jnp.zeros(table.shape, BF16)
     for time_tap in range(3):
         for row_tap in range(3):
@@ -183,12 +165,32 @@
                 into = row_tap * 2 * LANES + (0, 64, LANES)[time_tap]
                 into += ((0, 112, 96), (0, -16, -32), (0, 112, 96))[time_tap][col_tap]
                 table[pl.ds(into, 16), :] = win_ref[time_tap * 9 + row_tap * 3 + col_tap]
-    for other, lat_ref in enumerate(lat_refs):
-        from_row = lat_ref.shape[0] - per_source if other != 1 else cache_rows
-        value = lat_ref[pl.ds(from_row, per_source), :].astype(F32)
-        rows = pl.ds(pl.multiple_of((owner ^ other) * per_source, 8), per_source)
-        xs[0, rows, :] = value
-        xs[1, rows, :] = pltpu.roll(value, 64, 1)
+    for tap, copy in enumerate(copies):
+        copy.wait()
+        if tap % 3 == 2:
+            stores[tap // 3].start()
+    for store in stores:
+        store.wait()
+
+
+def new_frames(
+    bands, gain_ref, table, lat_ref, mid_ref, *refs,
+    owners, units, capacity, height, block, band_max, channels,
+):
+    group = lax.axis_index("seq")
+    owner = lax.axis_index("dec")
+    out_ref, part_ref, weights, xs, windows_a, windows_b, first_a, first_b = refs[:8]
+    act_a, act_b, late, out_sems, sem = refs[8:]
+    load = pltpu.make_async_copy(mid_ref, weights, sem)
+    load.start()
+    live = bands[group, owner]
+    start = band_start(bands, group, owner, owners)
+    edge = lax.rem(height - lax.rem(start - 1 + height, height), height)
+    blocks = band_max // block
+    size = F * COLS
+    per_source = lat_ref.shape[1]
+    for source in range(owners):
+        xs[pl.ds(source * per_source, per_source), :] = lat_ref[source].astype(F32)
     window_zero, act_zero = block + 4, block + 2
     for windows in (windows_a, windows_b):
         windows[window_zero] = jnp.zeros(windows.shape[1:], BF16)
@@ -216,11 +218,10 @@
         for frame in range(CT + F):
             for half in range(2):
                 at_row = pl.ds(base + half * (CT + F) + frame, 1)
-                for turn in range(2):
-                    if turn == 1 and not 1 <= frame <= F:
-                        continue
-                    value = jnp.broadcast_to(xs[turn, at_row, :], (8, LANES))
-                    rolled[turn][half, frame] = pltpu.roll(value, 0, 1, stride=16, stride_axis=0)
+                value = jnp.broadcast_to(xs[at_row, :], (8, LANES))
+                rolled[0][half, frame] = pltpu.roll(value, 0, 1, stride=16, stride_axis=0)
+                if 1 <= frame <= F:
+                    rolled[1][half, frame] = pltpu.roll(rolled[0][half, frame], 64, 1)
         for frame in range(F):
             pair = [
                 jnp.where(low, rolled[0][half, frame], rolled[1][half, frame + 1])
@@ -314,6 +315,7 @@
     fill_block(0, block + 2, windows_b)
     activate(convolve_first(0, block + 2, windows_b), block + 2, 0, first_a, act_a)
     fill_block(block + 2, block, windows_a)
+    load.wait()
     used = lax.div(live + block - 1, block)
 
     def two_steps(pair, carry):
@@ -483,24 +485,27 @@
         ]
 
     traded = trade(packed, "seq")
-    wide_mid, mark = pl.pallas_call(
+    wide_mid, table = pl.pallas_call(
         widen_weights,
-        in_specs=[in_hbm],
-        out_specs=[in_vmem, in_vmem],
-        scratch_shapes=[pltpu.SemaphoreType.DMA((27,))],
+        in_specs=[in_hbm, in_vmem],
+        out_specs=[in_hbm, in_vmem],
+        scratch_shapes=[
+            pltpu.VMEM((9 * channels, 3 * channels), BF16),
+            pltpu.SemaphoreType.DMA((27,)),
+            pltpu.SemaphoreType.DMA((9,)),
+        ],
         out_shape=[
             jax.ShapeDtypeStruct((9 * channels, 3 * channels), BF16),
-            jax.ShapeDtypeStruct((8, LANES), F32),
+            jax.ShapeDtypeStruct((6 * LANES, channels), BF16),
         ],
-        compiler_params=params(16),
+        compiler_params=params(50),
         cost_estimate=pl.CostEstimate(
             flops=0, bytes_accessed=4 * 27 * channels * channels, transcendentals=0
         ),
         name="widen_weights",
-    )(w_mid)
+    )(w_mid, w_in)
     lat_capacity = (band_max + 4 + owners - 1) // owners
     slice_rows = (lat_capacity * 12 + 15) // 16 * 16
-    slice_both = (act_capacity * tiles + slice_rows + tiles - 1) // tiles * tiles
     slice_act = jax.ShapeDtypeStruct((act_capacity * tiles, LANES), BF16)
     slice_two = jax.ShapeDtypeStruct((2 * act_capacity * tiles, LANES), BF16)
     sliced = pl.pallas_call(
@@ -511,8 +516,8 @@
         grid_spec=pltpu.PrefetchScalarGridSpec(
             num_scalar_prefetch=1,
             grid=(),
-            in_specs=[in_vmem] * (1 + clips),
-            out_specs=[in_vmem] * (2 * owners - 2),
+            in_specs=[any_space] + [in_vmem] * clips,
+            out_specs=[in_vmem] * owners,
             scratch_shapes=[
                 pltpu.VMEM((units * 12 + slice_rows, LANES), F32),
                 pltpu.VMEM((units * tiles, LANES), BF16),
@@ -521,38 +526,33 @@
             ],
         ),
         out_shape=[
-            jax.ShapeDtypeStruct((slice_both if other == 1 else slice_rows, LANES), BF16)
-            for other in range(owners)
+            jax.ShapeDtypeStruct((owners, slice_rows, LANES), BF16), slice_act, slice_act, slice_two
         ]
-        + [slice_act, slice_two]
         + [slice_act] * (owners - 4),
         compiler_params=params(16),
         name="slice_bands",
-    )(band_rows, mark, *traded)
-    band_lat, band_act = lax.optimization_barrier(
-        (trade(sliced[:owners], "dec"), sliced[owners:])
-    )
+    )(band_rows, table, *traded)
+    band_lat, own, beside, two, *far = sliced
+    band_lat = lax.all_to_all(band_lat, "dec", split_axis=0, concat_axis=0, tiled=True)
 
     def send(part, other):
         return lax.ppermute(part, "dec", [(i, i ^ other) for i in range(owners)])
 
-    own, *band_act = band_act
-    far = [send(part, other) for other, part in enumerate(band_act[1:], 4)]
-    two = send(band_act[0], 2)
-
-    late, part = pl.pallas_call(
+    far = [send(part, other) for other, part in enumerate(far, 4)]
+    two = send(two, 2)
+
+    late, part, weights = pl.pallas_call(
         functools.partial(
             new_frames, owners=owners, units=units, capacity=lat_capacity, height=height,
-            block=block, band_max=band_max, channels=channels, cache_rows=act_capacity * tiles,
+            block=block, band_max=band_max, channels=channels,
         ),
         grid_spec=pltpu.PrefetchScalarGridSpec(
             num_scalar_prefetch=1,
             grid=(),
-            in_specs=[in_vmem] * (3 + owners),
-            out_specs=[in_hbm, in_vmem],
+            in_specs=[in_vmem, in_vmem, in_vmem, in_hbm],
+            out_specs=[in_hbm, in_vmem, in_vmem],
             scratch_shapes=[
-                pltpu.VMEM((6 * LANES, channels), BF16),
-                pltpu.VMEM((2, owners * slice_rows, LANES), F32),
+                pltpu.VMEM((owners * slice_rows, LANES), F32),
                 pltpu.VMEM((block + 5, F * COLS, 2 * LANES), BF16),
                 pltpu.VMEM((block + 5, F * COLS, 2 * LANES), BF16),
                 pltpu.VMEM(((block + 2) * F * COLS, channels), F32),
@@ -561,11 +561,13 @@
                 pltpu.VMEM((block + 3, F, COLS, channels), BF16),
                 pltpu.VMEM((band_max, 2, COLS, channels), BF16),
                 pltpu.SemaphoreType.DMA((band_max // block,)),
+                pltpu.SemaphoreType.DMA,
             ],
         ),
         out_shape=[
             jax.ShapeDtypeStruct((band_max, F, COLS, channels), BF16),
             jax.ShapeDtypeStruct((band_max, 2, COLS, channels), F32),
+            jax.ShapeDtypeStruct((9 * channels, 3 * channels), BF16),
         ],
         compiler_params=params(36),
         cost_estimate=pl.CostEstimate(
@@ -574,12 +576,13 @@
             transcendentals=0,
         ),
         name="new_frames",
-    )(band_rows, w_in, norm_gain.reshape(1, channels), wide_mid, *band_lat)
+    )(band_rows, norm_gain.reshape(1, channels), table, band_lat, wide_mid)
 
     slots = owners * act_capacity
-    two, part = lax.optimization_barrier((two, part))
+    two, beside, part = lax.optimization_barrier((two, beside, part))
     handed = send(two[act_capacity * tiles :], 1)
-    band_act = [rows.reshape(-1, tiles, LANES) for rows in (own, band_lat[1], two, handed, *far)]
+    beside = send(beside, 1)
+    band_act = [rows.reshape(-1, tiles, LANES) for rows in (own, beside, two, handed, *far)]
     decoded = pl.pallas_call(
         functools.partial(
             cached_frames, owners=owners, units=units, capacity=act_capacity, height=height,
@@ -606,7 +609,7 @@
             transcendentals=0,
         ),
         name="cached_frames",
-    )(band_rows, part, wide_mid, late, *band_act)
+    )(band_rows, part, weights, late, *band_act)
     return decoded.reshape((1, 1) + decoded.shape)
 
 

time: 120 us -> 147 us (1.23)
  the two profiles are of different devices: /device:TPU:11 before, /device:TPU:30 now
where the time goes in v1:
time: 147 us; the launch traced here: 145 us
  Pallas kernels  90.5 us (62%)
  waiting for transfers between devices  37.5 us (26%)
  starting transfers between devices  15.5 us (11%)
    pallas_call x1, Pallas kernels, shards(): pl.pallas_call(functools.partial(new_frames, owners=owners, units=units,...  56.5 us
    all_to_all x1, waiting for transfers between devices, shards(): lax.all_to_all(band_lat, 'dec', split_axis=0, concat_axis=0, tiled=True)  29.8 us
    pallas_call x1, Pallas kernels, shards(): pl.pallas_call(functools.partial(cached_frames, owners=owners, units=unit...  19.7 us
    ppermute x7, starting transfers between devices, send(): return lax.ppermute(part, 'dec', [(i, i ^ other) for i in range(owners)])  6.82 us
    pallas_call x1, Pallas kernels, shards(): pl.pallas_call(widen_weights, in_specs=[in_hbm, in_vmem], out_specs=[in_h...  6.51 us
    ppermute x3, waiting for transfers between devices, trade(): lax.ppermute(part, axis, [(i, i ^ other) for i in range(count)])  6.12 us
    all_to_all x1, starting transfers between devices, shards(): lax.all_to_all(band_lat, 'dec', split_axis=0, concat_axis=0, tiled=True)  5.11 us
    pallas_call x1, Pallas kernels, shards(): pl.pallas_call(functools.partial(pack_clips, per_owner=per_owner, per_ste...  4.53 us
  transfers between devices with their start and end apart: 11, of which 4 were waited for; matrix products, arithmetic and copies ran while one was open for 0% of the time, Pallas kernels for 43%

profile of v1, /device:TPU:30, one launch (start us, length us, event | category | flops | bytes accessed | tf_op | source)
XLA Modules:
  0.0 144.8 jit_solution(4414583397076703957)
XLA Ops:
  0.0 4.5 %pack_clips.1 = (bf16[1296,128]{1,0:T(8,128)(2,1)}, bf16[1296,128]{1,0:T(8,128)(2,1)}, bf16[1296,128]{1,0:T(8,128)(2,1)}, bf16[1296,128]{1,0:T(8,128)(2,1)}) custom-call(s32[4,4]{1,0:T(4,128)} %groups_ref.1, bf16[12,4,1024]{2,1,0:T(4,128)(2,1)} %bitcast.24, bf16[12,4,512]{2,1,0:T(4,128)(2,1)} %bitcast.25, bf16[12,4,12288]{2,1,0:T(4,128)(2,1)} %bitcast.23), custom_call_target="tpu_custom_call" | custom-call | tf_op jit(solution)/shard_map/pack_clips/pallas_call | solution.py:456
  4.5 0.6 collective-permute-start
  5.1 0.5 collective-permute-start.1
  5.6 2.4 %collective-permute-start.2 = (bf16[1296,128]{1,0:T(8,128)(2,1)}, bf16[1296,128]{1,0:T(8,128)(2,1)S(1)}, u32[]{:S(2)}, u32[]{:S(2)}) collective-permute-start(bf16[1296,128]{1,0:T(8,128)(2,1)} %get-tuple-element.29), channel_id=1, source_target_pairs={{0,24},{8,16},{16,8},{24,0},{1,25},{9,17},{17,9},{25,1},{2,26},{10... | collective-permute-start | bytes 995336 | tf_op jit(solution)/shard_map/ppermute | solution.py:482
  8.1 1.0 copy-done
  9.1 6.5 %widen_weights.1 = (bf16[3456,1152]{1,0:T(8,128)(2,1)}, bf16[768,384]{1,0:T(8,128)(2,1)S(1)}) custom-call(bf16[27,384,384]{2,1,0:T(8,128)(2,1)} %mid_ref.1, bf16[27,16,384]{2,1,0:T(8,128)(2,1)S(1)} %copy-done), custom_call_target="tpu_custom_call" | custom-call | bytes 15925248 | tf_op jit(solution)/shard_map/widen_weights/pallas_call | solution.py:488
  15.6 0.0 collective-permute-done.refs_1_
  15.6 6.1 %collective-permute-done.1.refs_2_ = bf16[1296,128]{1,0:T(8,128)(2,1)S(1)} collective-permute-done((bf16[1296,128]{1,0:T(8,128)(2,1)}, bf16[1296,128]{1,0:T(8,128)(2,1)S(1)}, u32[]{:S(2)}, u32[]{:S(2)}) %collective-permute-start.1) | collective-permute-done | bytes 331808 | tf_op jit(solution)/shard_map/ppermute | solution.py:482
  21.7 3.4 %slice_bands.1 = (bf16[8,160,128]{2,1,0:T(8,128)(2,1)}, bf16[1248,128]{1,0:T(8,128)(2,1)S(1)}, bf16[1248,128]{1,0:T(8,128)(2,1)S(1)}, bf16[2496,128]{1,0:T(8,128...) custom-call(s32[4,8]{1,0:T(4,128)S(1)} %copy-done.2, ...), custom_call_target="tpu_custom_call" | custom-call | tf_op jit(solution)/shard_map/slice_bands/pallas_call | solution.py:511
  25.1 5.1 %all-to-all-start = ((bf16[8,160,128]{2,1,0:T(8,128)(2,1)}), bf16[8,160,128]{2,1,0:T(8,128)(2,1)S(1)}, u32[]{:S(2)}, u32[]{:S(2)}) async-start(bf16[8,160,128]{2,1,0:T(8,128)(2,1)} %get-tuple-element.32), calls=%async_computation | async-start | bytes 655360 | tf_op jit(solution)/shard_map/all_to_all | solution.py:536
  30.2 0.6 collective-permute-start.6
  30.8 1.8 %collective-permute-start.7 = (bf16[1248,128]{1,0:T(8,128)(2,1)}, bf16[1248,128]{1,0:T(8,128)(2,1)}, u32[]{:S(2)}, u32[]{:S(2)}) collective-permute-start(bf16[1248,128]{1,0:T(8,128)(2,1)} %get-tuple-element.42), channel_id=1, source_target_pairs={{0,5},{1,4},{2,7},{3,6},{4,1},{5,0},{6,3},{7,2},{8,13},{9,12},{10,... | collective-permute-start | bytes 958472 | tf_op jit(solution)/shard_map/ppermute | solution.py:539
  32.7 0.5 collective-permute-start.8
  33.2 3.3 %collective-permute-start.9 = (bf16[1248,128]{1,0:T(8,128)(2,1)S(1)}, bf16[1248,128]{1,0:T(8,128)(2,1)}, u32[]{:S(2)}, u32[]{:S(2)}) collective-permute-start(bf16[1248,128]{1,0:T(8,128)(2,1)S(1)} %get-tuple-element.44), channel_id=1, source_target_pairs={{0,7},{1,6},{2,5},{3,4},{4,3},{5,2},{6,1},{7,0},{8,15},{9,14},{10,... | collective-permute-start | bytes 958472 | tf_op jit(solution)/shard_map/ppermute | solution.py:539
  36.5 29.8 %all-to-all-done.lat_ref = bf16[8,160,128]{2,1,0:T(8,128)(2,1)S(1)} async-done(((bf16[8,160,128]{2,1,0:T(8,128)(2,1)}), bf16[8,160,128]{2,1,0:T(8,128)(2,1)S(1)}, u32[]{:S(2)}, u32[]{:S(2)}) %all-to-all-start) | async-done | bytes 327712 | tf_op jit(solution)/shard_map/all_to_all | solution.py:536
  66.3 56.5 %new_frames.1 = (bf16[96,4,16,384]{3,2,1,0:T(8,128)(2,1)}, f32[96,2,16,384]{3,2,1,0:T(8,128)S(1)}, bf16[3456,1152]{1,0:T(8,128)(2,1)S(1)}) custom-call(s32[4,8]{1,0:T(4,128)S(1)} %copy-done.2, f32[1,384]{1,0:T(1,128)S(1)} %reshape.30.gain_ref, bf16[768,384]{1,0:T(8,128)(2,1)S(1)} %get-tuple-element.25._.table, ...), custom_call_target="tpu_custom_call" | custom-call | flops 36691771392 | bytes 16777216 | tf_op jit(solution)/shard_map/new_frames/pallas_call | solution.py:544
  122.8 0.1 collective-permute-start.5
  122.9 0.5 collective-permute-start.4
  123.4 0.0 collective-permute-done.7
  123.4 0.0 collective-permute-done.8
  123.4 0.0 collective-permute-done.9
  123.4 1.1 collective-permute-done.5
  124.5 0.5 collective-permute-done.4
  125.0 19.7 %cached_frames.1 = bf16[96,4,16,384]{3,2,1,0:T(8,128)(2,1)} custom-call(s32[4,8]{1,0:T(4,128)S(1)} %copy-done.2, f32[96,2,16,384]{3,2,1,0:T(8,128)S(1)} %get-tuple-element.35.part_ref, bf16[3456,1152]{1,0:T(8,128)(2,1)S(1)} %get-tuple-element.36.weights, bf16[96,4,16,384]{3,2,1,0:T(8,128)(2,1)} %get-tuple-element.37.late_ref, ...), custom_call_target="tpu_custom_call", output_to_operand_aliasing={{}: (3, {})} | custom-call | flops 12230590464 | bytes 16777216 | tf_op jit(solution)/shard_map/cached_frames/pallas_call | solution.py:586
  (13 shorter events, 0.0 us)
Async XLA Ops:
  0.0 21.7 %copy-start.2 = (s32[4,8]{1,0:T(4,128)S(1)}, s32[4,8]{1,0:T(4,128)}, u32[]{:S(2)}) copy-start(s32[4,8]{1,0:T(4,128)} %bands.5) | copy-start | bytes 388
  4.5 11.1 %collective-permute-start = (bf16[1296,128]{1,0:T(8,128)(2,1)}, bf16[1296,128]{1,0:T(8,128)(2,1)S(1)}, u32[]{:S(2)}, u32[]{:S(2)}) collective-permute-start(bf16[1296,128]{1,0:T(8,128)(2,1)} %get-tuple-element.27), channel_id=1, source_target_pairs={{0,8},{8,0},{16,24},{24,16},{1,9},{9,1},{17,25},{25,17},{2,10},{10... | collective-permute-start | bytes 995336 | tf_op jit(solution)/shard_map/ppermute | solution.py:482
  5.1 16.6 %collective-permute-start.1 = (bf16[1296,128]{1,0:T(8,128)(2,1)}, bf16[1296,128]{1,0:T(8,128)(2,1)S(1)}, u32[]{:S(2)}, u32[]{:S(2)}) collective-permute-start(bf16[1296,128]{1,0:T(8,128)(2,1)} %get-tuple-element.28), channel_id=1, source_target_pairs={{0,16},{8,24},{16,0},{24,8},{1,17},{9,25},{17,1},{25,9},{2,18},{10... | collective-permute-start | bytes 995336 | tf_op jit(solution)/shard_map/ppermute | solution.py:482
  5.6 16.1 %collective-permute-start.2 = (bf16[1296,128]{1,0:T(8,128)(2,1)}, bf16[1296,128]{1,0:T(8,128)(2,1)S(1)}, u32[]{:S(2)}, u32[]{:S(2)}) collective-permute-start(bf16[1296,128]{1,0:T(8,128)(2,1)} %get-tuple-element.29), channel_id=1, source_target_pairs={{0,24},{8,16},{16,8},{24,0},{1,25},{9,17},{17,9},{25,1},{2,26},{10... | collective-permute-start | bytes 995336 | tf_op jit(solution)/shard_map/ppermute | solution.py:482
  8.1 1.0 copy-start
  9.1 12.7 %copy-start.1 = (bf16[1296,128]{1,0:T(8,128)(2,1)S(1)}, bf16[1296,128]{1,0:T(8,128)(2,1)}, u32[]{:S(2)}) copy-start(bf16[1296,128]{1,0:T(8,128)(2,1)} %get-tuple-element.26.refs_0_) | copy-start | bytes 995332
  9.1 21.1 %copy-start.3 = (f32[384]{0:T(512)S(1)}, f32[384]{0:T(512)}, u32[]{:S(2)}) copy-start(f32[384]{0:T(512)} %param.13) | copy-start | bytes 4612
  25.1 41.2 %all-to-all-start = ((bf16[8,160,128]{2,1,0:T(8,128)(2,1)}), bf16[8,160,128]{2,1,0:T(8,128)(2,1)S(1)}, u32[]{:S(2)}, u32[]{:S(2)}) async-start(bf16[8,160,128]{2,1,0:T(8,128)(2,1)} %get-tuple-element.32), calls=%async_computation | async-start | bytes 655360 | tf_op jit(solution)/shard_map/all_to_all | solution.py:536
  30.2 92.7 %collective-permute-start.6 = (bf16[1248,128]{1,0:T(8,128)(2,1)}, bf16[1248,128]{1,0:T(8,128)(2,1)S(1)}, u32[]{:S(2)}, u32[]{:S(2)}) collective-permute-start(bf16[1248,128]{1,0:T(8,128)(2,1)} %get-tuple-element.41), channel_id=1, source_target_pairs={{0,4},{1,5},{2,6},{3,7},{4,0},{5,1},{6,2},{7,3},{8,12},{9,13},{10,... | collective-permute-start | bytes 958472 | tf_op jit(solution)/shard_map/ppermute | solution.py:539
  30.8 92.6 %collective-permute-start.7 = (bf16[1248,128]{1,0:T(8,128)(2,1)}, bf16[1248,128]{1,0:T(8,128)(2,1)}, u32[]{:S(2)}, u32[]{:S(2)}) collective-permute-start(bf16[1248,128]{1,0:T(8,128)(2,1)} %get-tuple-element.42), channel_id=1, source_target_pairs={{0,5},{1,4},{2,7},{3,6},{4,1},{5,0},{6,3},{7,2},{8,13},{9,12},{10,... | collective-permute-start | bytes 958472 | tf_op jit(solution)/shard_map/ppermute | solution.py:539
  32.7 90.7 %collective-permute-start.8 = (bf16[1248,128]{1,0:T(8,128)(2,1)}, bf16[1248,128]{1,0:T(8,128)(2,1)}, u32[]{:S(2)}, u32[]{:S(2)}) collective-permute-start(bf16[1248,128]{1,0:T(8,128)(2,1)} %get-tuple-element.43), channel_id=1, source_target_pairs={{0,6},{1,7},{2,4},{3,5},{4,2},{5,3},{6,0},{7,1},{8,14},{9,15},{10,... | collective-permute-start | bytes 958472 | tf_op jit(solution)/shard_map/ppermute | solution.py:539
  33.2 90.2 %collective-permute-start.9 = (bf16[1248,128]{1,0:T(8,128)(2,1)S(1)}, bf16[1248,128]{1,0:T(8,128)(2,1)}, u32[]{:S(2)}, u32[]{:S(2)}) collective-permute-start(bf16[1248,128]{1,0:T(8,128)(2,1)S(1)} %get-tuple-element.44), channel_id=1, source_target_pairs={{0,7},{1,6},{2,5},{3,4},{4,3},{5,2},{6,1},{7,0},{8,15},{9,14},{10,... | collective-permute-start | bytes 958472 | tf_op jit(solution)/shard_map/ppermute | solution.py:539
  36.5 86.3 %collective-permute-start.3 = (bf16[2496,128]{1,0:T(8,128)(2,1)S(1)}, bf16[2496,128]{1,0:T(8,128)(2,1)S(1)}, u32[]{:S(2)}, u32[]{:S(2)}) collective-permute-start(bf16[2496,128]{1,0:T(8,128)(2,1)S(1)} %get-tuple-element.30), channel_id=1, source_target_pairs={{0,2},{1,3},{2,0},{3,1},{4,6},{5,7},{6,4},{7,5},{8,10},{9,11},{10,... | collective-permute-start | bytes 1916936 | tf_op jit(solution)/shard_map/ppermute | solution.py:539
  122.8 1.7 %collective-permute-start.5 = (bf16[1248,128]{1,0:T(8,128)(2,1)S(1)}, bf16[1248,128]{1,0:T(8,128)(2,1)S(1)}, u32[]{:S(2)}, u32[]{:S(2)}) collective-permute-start(bf16[1248,128]{1,0:T(8,128)(2,1)S(1)} %slice.3), channel_id=1, source_target_pairs={{0,1},{1,0},{2,3},{3,2},{4,5},{5,4},{6,7},{7,6},{8,9},{9,8},{10,11... | collective-permute-start | bytes 958472 | tf_op jit(solution)/shard_map/ppermute | solution.py:539
  122.9 2.1 %collective-permute-start.4 = (bf16[1248,128]{1,0:T(8,128)(2,1)S(1)}, bf16[1248,128]{1,0:T(8,128)(2,1)S(1)}, u32[]{:S(2)}, u32[]{:S(2)}) collective-permute-start(bf16[1248,128]{1,0:T(8,128)(2,1)S(1)} %get-tuple-element.39), channel_id=1, source_target_pairs={{0,1},{1,0},{2,3},{3,2},{4,5},{5,4},{6,7},{7,6},{8,9},{9,8},{10,11... | collective-permute-start | bytes 958472 | tf_op jit(solution)/shard_map/ppermute | solution.py:539
